TPU v7x, 128 devices: a whole 4x4x4 slice. The times are simulated.
128 devices in a mesh: gx: 8 (over z, core), gy: 4 (over y), gz: 4 (over x).
Axes of the slice: x: 4, y: 4, z: 4, core: 2. Of those that a mesh axis runs over, the one named last changes fastest.
Arguments:
- right_side: float32 [128, 128, 512], P('gx', 'gy', 'gz'), may hold values from -2.35 to 2.35
- initial: float32 [128, 128, 512], P('gx', 'gy', 'gz'), may hold values from -3 to 3
- alpha: float32 [128, 128, 512], P('gx', 'gy', 'gz'), may hold values from 0.0001 to 0.004
- beta_x: float32 [128, 128, 512], P('gx', 'gy', 'gz'), may hold values from 0.25 to 4
- beta_y: float32 [128, 128, 512], P('gx', 'gy', 'gz'), may hold values from 0.25 to 4
- beta_z: float32 [128, 128, 512], P('gx', 'gy', 'gz'), may hold values from 0.25 to 4
Outputs:
- solution_field: float32 [128, 128, 512], P('gx', 'gy', 'gz')
- residual: float32 [128, 128, 512], P('gx', 'gy', 'gz')
All inputs are finite; a program needn't handle non-finite values.
Results may differ from a plain program's by a relative error of at most 0.0003.
Values sent between devices are 32-bit elements; how exact they have to be, the bound alone decides.
A program may use at most 192 MiB of HBM per device.

v0:
```python
import itertools

import jax
import jax.numpy as jnp
from jax import lax
from jax.experimental import pallas as pl
from jax.experimental.pallas import tpu as pltpu
from jax.sharding import PartitionSpec as P

MESH = pl.DeviceIdType.MESH
F32 = jnp.float32
GRID = (8, 4, 4)
OFFS = [o for o in itertools.product((-1, 0, 1), repeat=3) if o != (0, 0, 0)]
FLAT = sorted([o for o in OFFS if o[2] == 0], key=lambda o: (o[0] != 0, o[1] == 0))
TALL = [o for o in OFFS if o[2] != 0]
RED, BLACK = 0, 1
SAME, OTHER_R, YL_R, YH_R, ZL_R, ZH_R, ID_R, D_R, OTHER_B, YL_B, YH_B, ZL_B, ZH_B, ID_B, D_B = range(15)


def dot(a, pick):
    total = None
    for _ in range(3):
        term = a.astype(jnp.bfloat16)
        part = jnp.dot(term, pick, preferred_element_type=F32)
        total = part if total is None else total + part
        a = a - term.astype(F32)
    return total


def iota(shape, dim):
    return lax.broadcasted_iota(jnp.int32, shape, dim)


def checker(shape):
    return ((iota(shape, 0) + iota(shape, 1)) & 1) == 0


def roll(x, shift, axis):
    size = x.shape[axis]
    shift = shift % size
    return pltpu.roll(x, shift, axis) if shift else x


def couplings(even, odd, next_x, keep_x, keep_next, keep_y, keep_z, scale, q0):
    parts = []
    for alpha, low_x, low_y, low_z in (even, odd):
        low_y, low_z = scale * low_y, scale * low_z
        own_y, own_z = low_y * keep_y, low_z * keep_z
        high_y, high_z = roll(own_y, -1, 0), roll(own_z, -1, 1)
        parts.append((own_y, high_y, own_z, high_z, alpha + (low_y + high_y) + (low_z + high_z)))
    x_e, x_o = scale * even[1], scale * odd[1]
    x_n = scale * next_x * keep_next
    d_e = parts[0][4] + (x_e + x_o)
    d_o = parts[1][4] + (x_o + x_n)
    x_e = x_e * keep_x
    i_e, i_o = 1.0 / d_e, 1.0 / d_o
    red = [jnp.where(q0, x_e, x_n)] + [jnp.where(q0, parts[0][n], parts[1][n]) for n in range(4)]
    red += [jnp.where(q0, i_e, i_o), jnp.where(q0, d_e, d_o)]
    black = [jnp.where(q0, x_n, x_e)] + [jnp.where(q0, parts[1][n], parts[0][n]) for n in range(4)]
    black += [jnp.where(q0, i_o, i_e), jnp.where(q0, d_o, d_e)]
    return [x_o] + red + black


def gathered_sum(colour, here, below, above, source, coef, q0):
    if colour == RED:
        other, base = jnp.where(q0, below, above), OTHER_R
    else:
        other, base = jnp.where(q0, above, below), OTHER_B
    total = source + coef(SAME) * here + coef(base) * other
    total = total + (coef(base + 1) * roll(here, 1, 0) + coef(base + 2) * roll(here, -1, 0))
    return total + (coef(base + 3) * roll(here, 1, 1) + coef(base + 4) * roll(here, -1, 1))


def kernel(
    f_hbm, u_hbm, a_hbm, bx_hbm, by_hbm, bz_hbm, sol, res,
    e5, y_top, y_bot, y_lo, y_hi, u_in, u0, s_hi, s_lo, l_lo, l_hi, k0, g0, r0, b0, u1, us, us_lo, us_hi,
    e1, e1s_up, e1s_dn, e1s_lo, e1s_hi, k1, f1, f1s, f1s_lo, f1s_hi, g1, r1, b1, v1, v1s, v1s_lo, v1s_hi,
    ga, gb, w2, k2, g2, r2, b2, k3, k4, work, work2, work3, mats, qz0,
    in_sem, a_send, a_recv, b_send, b_recv, c_send, c_recv, d_send, d_recv, e_send, e_recv,
    h_send, h_recv, p_send, p_recv, i_send, i_recv,
):
    gx, gy, gz = lax.axis_index("gx"), lax.axis_index("gy"), lax.axis_index("gz")
    me = (gx, gy, gz)
    core = lax.rem(gx, 2)
    chip = ((gx // 2) * 4 + gy) * 4 + gz

    def nb(o):
        return tuple(lax.rem(me[d] + (o[d] + GRID[d]), GRID[d]) if o[d] else me[d] for d in range(3))

    partner = (gx + 1 - 2 * core, gy, gz)

    loads = [pltpu.make_async_copy(u_hbm, u_in, in_sem.at[5])]
    for n, ref in enumerate((f_hbm, a_hbm, bx_hbm, by_hbm, bz_hbm)):
        loads.append(pltpu.make_async_copy(ref, e5.at[n, pl.ds(4, 16)], in_sem.at[n]))
    for c in loads:
        c.start()

    def zero(ref, at):
        ref[at] = jnp.zeros(ref.shape[1:], F32)

    for ref in (u0, u1):
        zero(ref, 0)
        zero(ref, 13)
    barrier = pltpu.get_barrier_semaphore()

    turns = [[lax.rem(at + k, 4) for k in range(4)] for at in (gx // 2, gy, gz)]
    peers = sorted(itertools.product(range(4), repeat=3), key=lambda k: -sum(min(n, 4 - n) for n in k))[:-1]
    peers = [(turns[0][k[0]] * 2 + core, turns[1][k[1]], turns[2][k[2]]) for k in peers]
    for to in peers:
        pl.semaphore_signal(barrier, inc=1, device_id=to, device_id_type=MESH)
    for o in OFFS:
        if o[0]:
            pl.semaphore_signal(barrier, inc=1, device_id=nb(o), device_id_type=MESH)

    row, col = iota((128, 128), 0), iota((128, 128), 1)
    one = lambda cond: jnp.where(cond, 1.0, 0.0).astype(F32)
    SUM, EVEN, SUM32, DOUBLE, TO1 = range(5)
    mats[SUM] = one((row >> 1) == (col & 63)).astype(jnp.bfloat16)
    mats[EVEN] = one(row == 2 * (col & 63)).astype(jnp.bfloat16)
    mats[SUM32] = one((row >> 1) == (col & 31)).astype(jnp.bfloat16)
    mats[DOUBLE] = one(row == (col >> 1)).astype(jnp.bfloat16)
    z1 = jnp.where(col < 96, col, col - 128)
    mats[TO1] = one(row == (((z1 + 64 * gz) >> 1) & 127)).astype(jnp.bfloat16)
    wide_col, wide_row = iota((128, 256), 1), iota((128, 256), 0)
    z0 = jnp.where(wide_col < 192, wide_col, wide_col - 256)
    qz0[...] = one(wide_row == ((z0 >> 1) & 127)).astype(jnp.bfloat16)

    q_l0 = checker((48, 256))
    q_in = checker((32, 128))
    q16 = checker((16, 128))
    q8 = checker((8, 128))
    lane8 = iota((8, 128), 1)
    lane16 = iota((16, 128), 1)
    lane32 = iota((32, 128), 1)
    lane48 = iota((48, 128), 1)
    first16 = (lane32 & 15) < 8
    first48 = (lane48 & 15) < 8

    for ref, at in ((r0, 0), (r0, 13), (b0, 0), (b0, 13), (r1, 0), (r1, 13), (b1, 0), (b1, 13)):
        zero(ref, at)
    for ref in (r2, b2):
        zero(ref, 0)
        zero(ref, 17)

    for c in loads:
        c.wait()

    def take_black(p, carry):
        u0[4 + p - 1, pl.ds(8, 32), pl.ds(0, 128)] = jnp.where(q_in, u_in[2 * p + 1], u_in[2 * p])
        return carry

    lax.fori_loop(0, 8, take_black, 0, unroll=2)

    sub8 = iota((8, 128), 0) < 4
    y_lo[:, 24] = jnp.zeros((3, 8, 128), F32)
    y_hi[:, 24] = jnp.zeros((3, 8, 128), F32)

    def take_ends(x, carry):
        for t, (n, k) in enumerate(((0, 1), (2, 4))):
            y_top[t, x] = jnp.where(sub8, roll(e5[n, 4 + x, pl.ds(24, 8), :], 4, 0), e5[k, 4 + x, pl.ds(24, 8), :])
            y_bot[t, x] = jnp.where(sub8, e5[n, 4 + x, pl.ds(0, 8), :], roll(e5[k, 4 + x, pl.ds(0, 8), :], 4, 0))
        y_top[2, x] = e5[3, 4 + x, pl.ds(24, 8), :]
        y_bot[2, x] = e5[3, 4 + x, pl.ds(0, 8), :]
        return carry

    lax.fori_loop(0, 16, take_ends, 0, unroll=4)

    pl.semaphore_wait(barrier, 81)

    def remote(src, dst, send, recv, to):
        return pltpu.make_async_remote_copy(
            src_ref=src, dst_ref=dst, send_sem=send, recv_sem=recv, device_id=to, device_id_type=MESH
        )

    Y0 = {-1: (8, 40, 8), 0: (8, 8, 32), 1: (32, 0, 8)}
    X5 = {-1: (0, 20, 5), 1: (12, 0, 4)}
    XY = {-1: (0, 20, 4), 0: (0, 4, 16), 1: (12, 0, 4)}
    XE = {-1: (3, 11, 2), 1: (9, 1, 2)}
    XU = {-1: (3, 11, 3), 0: (3, 3, 8), 1: (8, 0, 3)}
    XS = {-1: (0, 3, 1), 0: (0, 1, 2), 1: (1, 0, 1)}
    YS = {-1: (0, 40, 8), 0: (0, 8, 32), 1: (24, 0, 8)}
    first = []
    for n, o in enumerate(FLAT):
        if o[1]:
            (xs, xd, xn), (src, dst) = XY[o[0]], (y_top, y_lo) if o[1] == 1 else (y_bot, y_hi)
        else:
            (xs, xd, xn), (src, dst) = X5[o[0]], (e5, e5)
            xs += 4
        first.append(remote(
            src.at[:, pl.ds(xs, xn)], dst.at[:, pl.ds(xd, xn)], a_send.at[18 + n], a_recv.at[18 + n], nb(o)
        ))
        (xs, xd, xn), (ys, yd, yn) = (XE if o[0] and o[1] else XU)[o[0]], Y0[o[1]]
        first.append(remote(
            u0.at[pl.ds(xs, xn), pl.ds(ys, yn), pl.ds(0, 128)], u0.at[pl.ds(xd, xn), pl.ds(yd, yn), pl.ds(0, 128)],
            a_send.at[26 + n], a_recv.at[26 + n], nb(o),
        ))
    for c in first:
        c.start()

    for half in range(2):
        for t, (one_n, two_n) in enumerate(((0, 1), (2, 3), (4, 5))):
            acc_a = jnp.zeros((32, 128), F32)
            acc_b = jnp.zeros((32, 128), F32)
            for m in range(8):
                at = 8 * half + m
                rolled = roll(e5[one_n, 4 + at], 16 * m + 8, 1)
                acc_a = jnp.where((lane32 >> 4) == m, rolled, acc_a)
                if two_n < 5:
                    rolled = roll(e5[two_n, 4 + at], 16 * m + 16, 1)
                elif m < 4:
                    rolled = roll(u0[3 + 4 * half + m, pl.ds(8, 32), pl.ds(0, 128)], 16 * m + 16, 1)
                else:
                    continue
                acc_b = jnp.where((((lane32 + 120) & 127) >> 4) == m, rolled, acc_b)
            s_hi[t, half] = jnp.where(first16, acc_a, acc_b)
            s_lo[t, half] = jnp.where(first16, acc_b, acc_a)

    beyond = []
    for n, o in enumerate(TALL):
        (xs, xd, xn), (ys, yd, yn) = XS[o[0]], YS[o[1]]
        src, dst = (s_hi, l_lo) if o[2] == 1 else (s_lo, l_hi)
        beyond.append(remote(
            src.at[:, pl.ds(xs, xn), pl.ds(ys, yn)], dst.at[:, pl.ds(xd, xn), pl.ds(yd, yn)],
            a_send.at[n], a_recv.at[n], nb(o),
        ))
    for c in beyond:
        c.start()
    first += beyond

    def coarsen(count, rows, read):
        size = count * rows
        for p in range(count):
            for n in range(4):
                even = read(n, 2 * p)
                work[pl.ds(n * size + p * rows, rows), :] = even if n == 1 else even + read(n, 2 * p + 1)
        work2[pl.ds(0, 3 * size), :] = dot(work[pl.ds(0, 3 * size), :], mats[SUM])
        work2[pl.ds(3 * size, size), :] = dot(work[pl.ds(3 * size, size), :], mats[EVEN])

        def result(n, p):
            at = n * size + p * rows
            low = work2[pl.ds(at, rows // 2, stride=2), :]
            if n == 2:
                return 0.25 * low
            return (0.125 if n == 0 else 0.25) * (low + work2[pl.ds(at + 1, rows // 2, stride=2), :])

        return result

    got = coarsen(8, 32, lambda n, x: e5[n + 1, 4 + x])
    first16b = (lane16 & 15) < 8
    for n in range(0, 4, 2):
        acc_a = jnp.zeros((16, 128), F32)
        acc_b = jnp.zeros((16, 128), F32)
        for m in range(8):
            one_v, two_v = got(n, m), got(n + 1, m)
            e1[n // 2, 8 + m, pl.ds(8, 16), :] = jnp.where(lane16 < 64, one_v, two_v)
            acc_a = jnp.where((lane16 >> 4) == m, roll(one_v, 16 * m + 8, 1), acc_a)
            acc_b = jnp.where((((lane16 + 120) & 127) >> 4) == m, roll(two_v, 16 * m + 16, 1), acc_b)
        e1s_up[n // 2] = jnp.where(first16b, acc_a, acc_b)
        e1s_dn[n // 2] = jnp.where(first16b, acc_b, acc_a)

    Y1 = {-1: (8, 24, 8), 0: (8, 8, 16), 1: (16, 0, 8)}
    YT = {-1: (0, 24, 8), 0: (0, 8, 16), 1: (8, 0, 8)}
    XT = {-1: 2, 0: 1, 1: 0}

    def spread1(main, to_high, to_low, low, high, send, recv, lead):
        out = []
        for n, o in enumerate(TALL):
            ys, yd, yn = YT[o[1]]
            dst, strip = (low, to_high) if o[2] == 1 else (high, to_low)
            src = strip.at[:, pl.ds(ys, yn)] if lead else strip.at[pl.ds(ys, yn)]
            dst = dst.at[:, XT[o[0]], pl.ds(yd, yn)] if lead else dst.at[XT[o[0]], pl.ds(yd, yn)]
            out.append(remote(src, dst, send.at[n], recv.at[n], nb(o)))
        for n, o in enumerate(FLAT):
            size = main.shape[1 if lead else 0] // 3
            (xs, xd, xn), (ys, yd, yn) = (size, size * (1 - o[0]), size), Y1[o[1]]
            src = (pl.ds(xs, xn), pl.ds(ys, yn))
            dst = (pl.ds(xd, xn), pl.ds(yd, yn))
            if lead:
                src, dst = (slice(None),) + src, (slice(None),) + dst
            out.append(remote(main.at[src], main.at[dst], send.at[18 + n], recv.at[18 + n], nb(o)))
        return out

    coefs1 = spread1(e1, e1s_up, e1s_dn, e1s_lo, e1s_hi, b_send, b_recv, True)
    for c in coefs1:
        c.start()

    def twice(n, value):
        other = roll(value, 64, 1)
        return jnp.where(lane16 < 64, other, value) if n % 2 else jnp.where(lane16 < 64, value, other)

    got = coarsen(4, 16, lambda n, x: twice(n, e1[n // 2, 8 + x, pl.ds(8, 16), :]))
    for n in range(4):
        acc = got(n, 0)
        for m in range(1, 4):
            acc = jnp.where((lane8 >> 5) == m, got(n, m), acc)
        ga[core, gx // 2, gy, gz, n] = acc

    def along(axis, k):
        if axis == "z":
            return lax.rem(gx + 2 * k, 8), gy, gz
        return (gx, lax.rem(gy + k, 4), gz) if axis == "y" else (gx, gy, lax.rem(gz + k, 4))

    def part(order, axis, back):
        z, y, x = gx // 2, gy, gz
        if axis == "z":
            z = lax.rem(z + 4 - back, 4)
        elif axis == "y":
            y = lax.rem(y + 4 - back, 4)
        else:
            x = lax.rem(x + 4 - back, 4)
        if order == "xyz":
            y, x = slice(None) if axis == "z" else y, x if axis == "x" else slice(None)
            return ga.at[core, z, y, x, pl.ds(0, 2)]
        z, y = slice(None) if axis == "x" else z, y if axis == "y" else slice(None)
        return ga.at[core, z, y, x, pl.ds(2, 2)]

    def legs(stage):
        for n, order in enumerate(("xyz", "yzx")):
            for k in range(1, 4):
                yield order, order[stage], k, 6 * stage + 3 * n + k - 1

    def pass_on(stage):
        for order, axis, k, at in legs(stage):
            own = part(order, axis, 0)
            remote(own, own, h_send.at[at], h_recv.at[at], along(axis, k)).start()

    def passed_on(stage):
        for order, axis, k, at in legs(stage):
            own, theirs = part(order, axis, 0), part(order, axis, k)
            remote(own, own, h_send.at[at], h_recv.at[at], along(axis, k)).wait_send()
            remote(theirs, theirs, h_send.at[at], h_recv.at[at], along(axis, k)).wait_recv()

    pass_on(0)
    passed_on(0)
    pass_on(1)

    for c in first:
        c.wait_recv()
    keep_y0 = one(((iota((48, 256), 0) - 8 + 32 * gy) & 127) != 0)
    lane256 = iota((48, 256), 1)
    keep_z0 = one(((jnp.where(lane256 < 192, lane256, lane256 - 256) + 128 * gz) & 511) != 0)

    def side(n, group, m):
        t, low, high = n // 2, l_lo, l_hi
        if n % 2:
            return pltpu.roll(jnp.where(first48, high[t, group], low[t, group]), lax.rem(112 - 16 * m + 128, 128), 1)
        return pltpu.roll(jnp.where(first48, low[t, group], high[t, group]), lax.rem(120 - 16 * m + 128, 128), 1)

    def fine_row(n, x):
        at = x + 4
        t, swap = ((0, 0), (0, 4), (1, 0), (2, 0), (1, 4))[n]
        low = y_lo[t, x] if swap or n == 3 else roll(y_lo[t, x], 4, 0)
        high = roll(y_hi[t, x], 4, 0) if swap else y_hi[t, x]
        main = jnp.concatenate([low, e5[n, x], high], axis=0)
        return jnp.concatenate([main, side(n, at // 8, lax.rem(at, 8))], axis=1)

    def build0(p, carry):
        e, o = 2 * p, 2 * p + 1
        even = tuple(fine_row(n, e) for n in range(1, 5))
        odd = tuple(fine_row(n, o) for n in range(1, 5))
        keep_e = jnp.where(((e - 4 + 16 * gx) & 127) == 0, 0.0, 1.0).astype(F32)
        keep_n = jnp.where(((e - 2 + 16 * gx) & 127) == 0, 0.0, 1.0).astype(F32)
        for n, value in enumerate(couplings(even, odd, fine_row(2, e + 2), keep_e, keep_n, keep_y0, keep_z0, 1.0, q_l0)):
            k0[n, p] = value
        f_e, f_o = fine_row(0, e), fine_row(0, o)
        g0[RED, p] = jnp.where(q_l0, f_e, f_o)
        g0[BLACK, p] = jnp.where(q_l0, f_o, f_e)
        return carry

    lax.fori_loop(0, 12, build0, 0, unroll=2)

    passed_on(1)
    pass_on(2)

    def side_u(p, carry):
        at = p + 1
        u0[p, :, pl.ds(128, 128)] = side(5, at // 4, lax.rem(at, 4))
        return carry

    lax.fori_loop(0, 14, side_u, 0, unroll=7)

    def half0(colour, src, dst, start, stop):
        def one_pair(p, carry):
            coef = lambda n: k0[n, p]
            total = gathered_sum(colour, src[p + 1], src[p], src[p + 2], g0[colour, p], coef, q_l0)
            dst[p + 1] = total * k0[ID_R if colour == RED else ID_B, p]
            return carry

        lax.fori_loop(start, stop, one_pair, 0, unroll=2)

    half0(RED, u0, r0, 0, 12)
    half0(BLACK, r0, b0, 0, 12)
    half0(RED, b0, r0, 1, 11)
    half0(BLACK, r0, b0, 1, 11)

    def resid0(p):
        coef = lambda n: k0[n, p]
        out = []
        for colour, own, far in ((RED, r0, b0), (BLACK, b0, r0)):
            total = gathered_sum(colour, far[p + 1], far[p], far[p + 2], g0[colour, p], coef, q_l0)
            out.append(total - k0[D_R if colour == RED else D_B, p] * own[p + 1])
        return out

    def restrict0(p, carry):
        red, black = resid0(p + 2)
        work[pl.ds(32 * p, 32), :] = (red + black)[8:40, :128]
        return carry

    lax.fori_loop(0, 8, restrict0, 0, unroll=2)
    work2[pl.ds(0, 256), :] = dot(work[pl.ds(0, 256), :], mats[SUM])
    acc = jnp.zeros((16, 128), F32)
    values = []
    for m in range(8):
        value = 0.125 * (work2[pl.ds(32 * m, 16, stride=2), :] + work2[pl.ds(32 * m + 1, 16, stride=2), :])
        values.append(value)
        if m >= 4:
            f1[m, pl.ds(8, 16), :] = jnp.where(lane16 < 64, values[m - 4], value)
        acc = jnp.where((lane16 >> 4) == m, roll(value, 16 * m + 8, 1), acc)
    f1s[...] = acc

    right1 = spread1(f1, f1s, f1s, f1s_lo, f1s_hi, c_send, c_recv, False)
    for c in right1:
        c.start()

    acc = jnp.zeros((32, 128), F32)
    for m in range(8):
        acc = jnp.where((lane32 >> 4) == m, roll(b0[3 + m, pl.ds(8, 32), pl.ds(0, 128)], 16 * m + 8, 1), acc)
    us[...] = acc
    YU = {-1: (0, 40, 8), 0: (0, 8, 32), 1: (24, 0, 8)}
    fine = []
    for n, o in enumerate(TALL):
        ys, yd, yn = YU[o[1]]
        dst = us_lo if o[2] == 1 else us_hi
        fine.append(remote(us.at[pl.ds(ys, yn)], dst.at[XT[o[0]], pl.ds(yd, yn)], d_send.at[n], d_recv.at[n], nb(o)))
    for n, o in enumerate(FLAT):
        (xs, xd, xn), (ys, yd, yn) = (XE if o[0] and o[1] else XU)[o[0]], Y0[o[1]]
        fine.append(remote(
            b0.at[pl.ds(xs, xn), pl.ds(ys, yn), pl.ds(0, 128)], u1.at[pl.ds(xd, xn), pl.ds(yd, yn), pl.ds(0, 128)],
            d_send.at[18 + n], d_recv.at[18 + n], nb(o),
        ))
    for c in fine:
        c.start()

    for c in first:
        c.wait_send()
    for c in coefs1:
        c.wait()
    keep_y1 = one(((iota((32, 128), 0) - 8 + 16 * gy) & 63) != 0)
    keep_z1 = one(((jnp.where(lane32 < 96, lane32, lane32 - 128) + 64 * gz) & 255) != 0)

    def joined(main, low, high, m, back=0):
        above = pltpu.roll(high, lax.rem(56 - back - 16 * m + 256, 128), 1)
        below = pltpu.roll(low, lax.rem(120 - back - 16 * m + 256, 128), 1)
        return jnp.where(lane32 < 64, main, jnp.where(lane32 < 96, above, below))

    def coarse_row(n, x):
        main = e1[n // 2, x]
        if n % 2:
            main = roll(main, 64, 1)
        return joined(main, e1s_lo[n // 2, x // 8], e1s_hi[n // 2, x // 8], lax.rem(x, 8), 8 * (n % 2))

    def build1(p, carry):
        e, o = 2 * p, 2 * p + 1
        even = tuple(coarse_row(n, e) for n in range(4))
        odd = tuple(coarse_row(n, o) for n in range(4))
        after = coarse_row(1, lax.rem(e + 2, 24))
        keep_e = jnp.where(((e - 8 + 8 * gx) & 63) == 0, 0.0, 1.0).astype(F32)
        keep_n = jnp.where(((e - 6 + 8 * gx) & 63) == 0, 0.0, 1.0).astype(F32)
        for n, value in enumerate(couplings(even, odd, after, keep_e, keep_n, keep_y1, keep_z1, 0.25, q_in)):
            k1[n, p] = value
        return carry

    lax.fori_loop(0, 12, build1, 0, unroll=2)

    passed_on(2)
    pair_a = remote(ga.at[core], ga.at[core], p_send.at[0], p_recv.at[0], partner)
    pair_a.start()

    for c in right1:
        c.wait_recv()

    def source1(p, carry):
        e, o = 2 * p, 2 * p + 1
        f_e, f_o = (
            joined(pltpu.roll(f1[(x // 8) * 4 + lax.rem(x, 4)], 64 * (lax.rem(x, 8) // 4), 1),
                   f1s_lo[x // 8], f1s_hi[x // 8], lax.rem(x, 8))
            for x in (e, o)
        )
        red = jnp.where(q_in, f_e, f_o)
        g1[RED, p] = red
        g1[BLACK, p] = jnp.where(q_in, f_o, f_e)
        r1[p + 1] = red * k1[ID_R, p]
        return carry

    lax.fori_loop(0, 12, source1, 0, unroll=4)

    def half1(colour, src, dst):
        def one_pair(p, carry):
            coef = lambda n: k1[n, p]
            total = gathered_sum(colour, src[p + 1], src[p], src[p + 2], g1[colour, p], coef, q_in)
            dst[p + 1] = total * k1[ID_R if colour == RED else ID_B, p]
            return carry

        lax.fori_loop(0, 12, one_pair, 0, unroll=6)

    half1(BLACK, r1, b1)
    half1(RED, b1, r1)
    half1(BLACK, r1, b1)
    for p in range(4):
        coef = lambda n: k1[n, p + 4]
        total = gathered_sum(RED, b1[p + 5], b1[p + 4], b1[p + 6], g1[RED, p + 4], coef, q_in) - k1[D_R, p + 4] * r1[p + 5]
        other = gathered_sum(BLACK, r1[p + 5], r1[p + 4], r1[p + 6], g1[BLACK, p + 4], coef, q_in)
        total = total + (other - k1[D_B, p + 4] * b1[p + 5])
        work[pl.ds(16 * p, 16), :] = jnp.where(lane16 < 64, total[8:24], 0.0)
    work2[pl.ds(0, 64), :] = dot(work[pl.ds(0, 64), :], mats[SUM32])
    acc = jnp.zeros((8, 128), F32)
    for m in range(4):
        value = 0.125 * (work2[pl.ds(16 * m, 8, stride=2), :] + work2[pl.ds(16 * m + 1, 8, stride=2), :])
        acc = jnp.where((lane8 >> 5) == m, value, acc)
    gb[core, chip] = acc

    for to in peers:
        remote(gb.at[core, chip], gb.at[core, chip], i_send.at[0], i_recv.at[0], to).start()

    acc = jnp.zeros((16, 128), F32)
    for m in range(4):
        value = b1[5 + m, pl.ds(8, 16), :]
        value = jnp.where(lane16 < 64, value, roll(value, 64, 1))
        acc = jnp.where((lane16 >> 4) == m, roll(value, 16 * m + 8, 1), acc)
        v1[4 + m, pl.ds(8, 16), :] = value
    v1s[...] = acc
    black1 = []
    for n, o in enumerate(TALL):
        ys, yd, yn = YT[o[1]]
        dst = v1s_lo if o[2] == 1 else v1s_hi
        black1.append(remote(v1s.at[pl.ds(ys, yn)], dst.at[XT[o[0]], pl.ds(yd, yn)], e_send.at[n], e_recv.at[n], nb(o)))
    for n, o in enumerate(FLAT):
        (xs, xd, xn), (ys, yd, yn) = {-1: (4, 8, 4), 0: (4, 4, 4), 1: (4, 0, 4)}[o[0]], Y1[o[1]]
        black1.append(remote(
            v1.at[pl.ds(xs, xn), pl.ds(ys, yn)], v1.at[pl.ds(xd, xn), pl.ds(yd, yn)],
            e_send.at[18 + n], e_recv.at[18 + n], nb(o),
        ))
    for c in black1:
        c.start()

    for c in right1:
        c.wait_send()

    pair_a.wait()

    def untile(tiles):
        out = []
        for m in range(4):
            total = tiles[0] if m == 0 else roll(tiles[0], -32 * m, 1)
            for k in range(1, 4):
                total = jnp.where((lane8 >> 5) == k, roll(tiles[k], 32 * (k - m), 1), total)
            out.append(total)
        return out

    def place(tiles_of, count):
        def one_block(t, carry):
            bx, by = t // 4, lax.rem(t, 4)
            rows = pl.ds(pl.multiple_of(8 * by, 8), 8)
            for n in range(count):
                for m, value in enumerate(untile([tiles_of(lax.rem(bx, 2), bx // 2, by, k, n) for k in range(4)])):
                    w2[n, 4 * bx + m, rows, :] = value
            return carry

        lax.fori_loop(0, 32, one_block, 0, unroll=4)

    place(lambda side_core, bz, by, k, n: ga[side_core, bz, by, k, n], 4)

    keep_y2 = one(iota((32, 128), 0) != 0)
    keep_z2 = one(lane32 != 0)

    def build2(p, carry):
        e, o = 2 * p, 2 * p + 1
        even = tuple(w2[n, e] for n in range(4))
        odd = tuple(w2[n, o] for n in range(4))
        keep_e = jnp.where(p == 0, 0.0, 1.0).astype(F32)
        keep_n = jnp.where(p == 15, 0.0, 1.0).astype(F32)
        after = w2[1, lax.rem(e + 2, 32)]
        for n, value in enumerate(couplings(even, odd, after, keep_e, keep_n, keep_y2, keep_z2, 0.25**2, q_in)):
            k2[n, p] = value
        return carry

    lax.fori_loop(0, 16, build2, 0, unroll=2)

    def small(level_coefs, count, rows, period, scale, q, dest):
        keep_y = one(iota((rows, 128), 0) != 0)
        keep_z = one((iota((rows, 128), 1) & (period - 1)) != 0)
        for p in range(count):
            even = tuple(level_coefs(n, 2 * p) for n in range(4))
            odd = tuple(level_coefs(n, 2 * p + 1) for n in range(4))
            after = level_coefs(1, (2 * p + 2) % (2 * count))
            for n, value in enumerate(couplings(
                even, odd, after, 0.0 if p == 0 else 1.0, 0.0 if p == count - 1 else 1.0, keep_y, keep_z, scale, q
            )):
                dest[n, p] = value

    got3 = coarsen(16, 32, lambda n, x: w2[n, x])
    rows3 = [[got3(n, x) for x in range(16)] for n in range(4)]
    for n in range(4):
        for x in range(16):
            w2[n, x, pl.ds(0, 16), :] = rows3[n][x]
    small(lambda n, x: w2[n, x, pl.ds(0, 16), :], 8, 16, 64, 0.25**3, q16, k3)
    got4 = coarsen(8, 16, lambda n, x: w2[n, x, pl.ds(0, 16), :])
    small(got4, 4, 8, 32, 0.25**4, q8, k4)

    others = gb.at[core, pl.ds(0, 63)]
    remote(others, others, i_send.at[0], i_recv.at[0], partner).wait()
    pair_b = remote(gb.at[core], gb.at[core], p_send.at[1], p_recv.at[1], partner)
    pair_b.start()
    pair_b.wait()

    place(lambda side_core, bz, by, k, n: gb[side_core, bz * 16 + by * 4 + k], 1)

    def source2(p, carry):
        f_e, f_o = w2[0, 2 * p], w2[0, 2 * p + 1]
        red = jnp.where(q_in, f_e, f_o)
        g2[RED, p] = red
        g2[BLACK, p] = jnp.where(q_in, f_o, f_e)
        r2[p + 1] = red * k2[ID_R, p]
        return carry

    lax.fori_loop(0, 16, source2, 0, unroll=2)

    def half2(colour, src, dst):
        def one_pair(p, carry):
            coef = lambda n: k2[n, p]
            total = gathered_sum(colour, src[p + 1], src[p], src[p + 2], g2[colour, p], coef, q_in)
            dst[p + 1] = total * k2[ID_R if colour == RED else ID_B, p]
            return carry

        lax.fori_loop(0, 16, one_pair, 0, unroll=8)

    half2(BLACK, r2, b2)
    half2(RED, b2, r2)
    half2(BLACK, r2, b2)

    def restrict2(p, carry):
        coef = lambda n: k2[n, p]
        total = gathered_sum(RED, b2[p + 1], b2[p], b2[p + 2], g2[RED, p], coef, q_in) - k2[D_R, p] * r2[p + 1]
        other = gathered_sum(BLACK, r2[p + 1], r2[p], r2[p + 2], g2[BLACK, p], coef, q_in)
        work[pl.ds(pl.multiple_of(32 * p, 32), 32), :] = total + (other - k2[D_B, p] * b2[p + 1])
        return carry

    lax.fori_loop(0, 16, restrict2, 0, unroll=4)
    work2[pl.ds(0, 512), :] = dot(work[pl.ds(0, 512), :], mats[SUM])

    def pack(rows, q):
        count = len(rows) // 2
        red = [jnp.where(q, rows[2 * p], rows[2 * p + 1]) for p in range(count)]
        black = [jnp.where(q, rows[2 * p + 1], rows[2 * p]) for p in range(count)]
        return red, black

    def half_small(colour, src, source, k, q, own=None):
        count = len(src)
        out = []
        for p in range(count):
            coef = lambda n: k[n, p]
            total = gathered_sum(colour, src[p], src[p - 1], src[(p + 1) % count], source[p], coef, q)
            if own is None:
                out.append(total * k[ID_R if colour == RED else ID_B, p])
            else:
                out.append(total - k[D_R if colour == RED else D_B, p] * own[p])
        return out

    def paired(count, rows):
        return [
            0.125 * (work2[pl.ds(2 * rows * m, rows, stride=2), :] + work2[pl.ds(2 * rows * m + 1, rows, stride=2), :])
            for m in range(count)
        ]

    def unpacked(red, black, q):
        out = []
        for r, b in zip(red, black):
            out += [jnp.where(q, r, b), jnp.where(q, b, r)]
        return out

    fr3, fb3 = pack(paired(16, 16), q16)
    r3 = [fr3[p] * k3[ID_R, p] for p in range(8)]
    b3 = half_small(BLACK, r3, fb3, k3, q16)
    r3 = half_small(RED, b3, fr3, k3, q16)
    b3 = half_small(BLACK, r3, fb3, k3, q16)
    left_r = half_small(RED, b3, fr3, k3, q16, r3)
    left_b = half_small(BLACK, r3, fb3, k3, q16, b3)
    for p in range(8):
        work[pl.ds(16 * p, 16), :] = left_r[p] + left_b[p]
    work2[pl.ds(0, 128), :] = dot(work[pl.ds(0, 128), :], mats[SUM])

    fr4, fb4 = pack(paired(8, 8), q8)
    r4 = [fr4[p] * k4[ID_R, p] for p in range(4)]
    b4 = half_small(BLACK, r4, fb4, k4, q8)

    def bottom(step, carry):
        black = list(carry[4:])
        red = half_small(RED, black, fr4, k4, q8)
        black = half_small(BLACK, red, fb4, k4, q8)
        return tuple(red + black)

    done = lax.fori_loop(0, 11, bottom, tuple(r4 + b4))
    e4 = unpacked(done[:4], done[4:], q8)

    def doubled(rows, size):
        total = 2 * size * len(rows)
        for m, value in enumerate(rows):
            work[pl.ds(2 * size * m, size, stride=2), :] = value
            work[pl.ds(2 * size * m + 1, size, stride=2), :] = value
        work2[pl.ds(0, total), :] = dot(work[pl.ds(0, total), :], mats[DOUBLE])
        return [work2[pl.ds(2 * size * m, 2 * size), :] for m in range(len(rows))]

    up3 = doubled(e4, 8)
    b3 = [b3[p] + up3[p] for p in range(8)]
    r3 = half_small(RED, b3, fr3, k3, q16)
    b3 = half_small(BLACK, r3, fb3, k3, q16)
    r3 = half_small(RED, b3, fr3, k3, q16)
    b3 = half_small(BLACK, r3, fb3, k3, q16)
    up2 = doubled(unpacked(r3, b3, q16), 16)
    for p in range(16):
        b2[p + 1] = b2[p + 1] + up2[p]

    half2(RED, b2, r2)
    half2(BLACK, r2, b2)
    half2(RED, b2, r2)
    half2(BLACK, r2, b2)

    for c in black1:
        c.wait()

    turn = (4 - 8 * gy) & 31
    for p in range(12):
        x = (p - 4 + 4 * gx) & 31
        red, black = r2[x // 2 + 1], b2[x // 2 + 1]
        lower = jnp.where((x & 1) == 0, 1, 0) == jnp.where(q_in, 1, 0)
        value = pltpu.roll(jnp.where(lower, red, black), turn, 0)[:16]
        work[pl.ds(32 * p, 16, stride=2), :] = value
        work[pl.ds(32 * p + 1, 16, stride=2), :] = value
    work2[pl.ds(0, 384), :] = dot(work[pl.ds(0, 384), :], mats[TO1])

    def lift1(p, carry):
        value = joined(v1[p], v1s_lo[p // 4], v1s_hi[p // 4], lax.rem(p, 4))
        b1[p + 1] = value + work2[pl.ds(pl.multiple_of(32 * p, 32), 32), :]
        return carry

    lax.fori_loop(0, 12, lift1, 0, unroll=4)
    half1(RED, b1, r1)
    half1(BLACK, r1, b1)
    half1(RED, b1, r1)
    half1(BLACK, r1, b1)

    for c in fine:
        c.wait()
    used = (lane32 < 72) | (lane32 >= 120)

    for p in range(14):
        x = p + 5
        red, black = r1[x // 2 + 1], b1[x // 2 + 1]
        value = jnp.where(q_in, red, black) if x % 2 == 0 else jnp.where(q_in, black, red)
        value = jnp.where(used, value, 0.0)[4:28]
        work[pl.ds(48 * p, 24, stride=2), :] = value
        work[pl.ds(48 * p + 1, 24, stride=2), :] = value
    work3[...] = dot(work[pl.ds(0, 672), :], qz0[...])

    def lift_halo(p, carry):
        at = p + 5
        group, m = at // 8, lax.rem(at, 8)
        merged = jnp.where(first48, us_lo[group], us_hi[group])
        beyond = pltpu.roll(merged, lax.rem(120 - 16 * m + 128, 128), 1)
        u1[p] = jnp.concatenate([u1[p, :, pl.ds(0, 128)], beyond], axis=1) + work3[pl.ds(pl.multiple_of(48 * p, 16), 48), :]
        return carry

    def own_black(p, carry):
        u1[p, pl.ds(8, 32), pl.ds(0, 128)] = b0[p, pl.ds(8, 32), pl.ds(0, 128)]
        return carry

    lax.fori_loop(3, 11, own_black, 0)
    lax.fori_loop(0, 14, lift_halo, 0, unroll=2)
    half0(RED, u1, r0, 0, 12)
    half0(BLACK, r0, b0, 0, 12)
    half0(RED, b0, r0, 1, 11)
    half0(BLACK, r0, b0, 1, 11)

    def finish(p, carry):
        red, black = resid0(p + 2)
        red, black = red[8:40, :128], black[8:40, :128]
        res[2 * p] = jnp.where(q_in, red, black)
        res[2 * p + 1] = jnp.where(q_in, black, red)
        red, black = r0[p + 3, pl.ds(8, 32), pl.ds(0, 128)], b0[p + 3, pl.ds(8, 32), pl.ds(0, 128)]
        sol[2 * p] = jnp.where(q_in, red, black)
        sol[2 * p + 1] = jnp.where(q_in, black, red)
        return carry

    lax.fori_loop(0, 8, finish, 0, unroll=2)


def on_device(right_side, initial, alpha, beta_x, beta_y, beta_z):
    block = jax.ShapeDtypeStruct(right_side.shape, F32)
    V = lambda *shape: pltpu.VMEM(shape, F32)
    D = lambda n: pltpu.SemaphoreType.DMA((n,))
    scratch = [
        V(5, 26, 32, 128), V(3, 16, 8, 128), V(3, 16, 8, 128), V(3, 25, 8, 128), V(3, 25, 8, 128),
        V(16, 32, 128), V(14, 48, 256),
        V(3, 2, 32, 128), V(3, 2, 32, 128), V(3, 4, 48, 128), V(3, 4, 48, 128),
        V(15, 12, 48, 256), V(2, 12, 48, 256), V(14, 48, 256), V(14, 48, 256), V(14, 48, 256),
        V(32, 128), V(3, 48, 128), V(3, 48, 128),
        V(2, 24, 32, 128), V(2, 16, 128), V(2, 16, 128), V(2, 3, 32, 128), V(2, 3, 32, 128), V(15, 12, 32, 128),
        V(12, 32, 128), V(16, 128), V(3, 32, 128), V(3, 32, 128),
        V(2, 12, 32, 128), V(14, 32, 128), V(14, 32, 128),
        V(12, 32, 128), V(16, 128), V(3, 32, 128), V(3, 32, 128),
        V(2, 4, 4, 4, 4, 8, 128), V(2, 64, 8, 128), V(4, 32, 32, 128), V(15, 16, 32, 128), V(2, 16, 32, 128),
        V(18, 32, 128), V(18, 32, 128), V(15, 8, 16, 128), V(15, 4, 8, 128),
        V(2048, 128), V(2048, 128), V(672, 256), pltpu.VMEM((5, 128, 128), jnp.bfloat16), pltpu.VMEM((128, 256), jnp.bfloat16),
        D(6), D(34), D(34), D(26), D(26), D(26), D(26), D(26), D(26), D(26), D(26),
        D(18), D(18), D(2), D(2), D(1), D(1),
    ]
    return pl.pallas_call(
        kernel,
        out_shape=(block, block),
        in_specs=[pl.BlockSpec(memory_space=pl.ANY)] * 6,
        out_specs=[pl.BlockSpec(memory_space=pltpu.VMEM)] * 2,
        scratch_shapes=scratch,
        compiler_params=pltpu.CompilerParams(collective_id=0, has_side_effects=True, vmem_limit_bytes=60 << 20),
    )(right_side, initial, alpha, beta_x, beta_y, beta_z)


def solution(mesh):
    spec = P("gx", "gy", "gz")
    return jax.shard_map(on_device, mesh=mesh, in_specs=(spec,) * 6, out_specs=(spec, spec), check_vma=False)
```

profile of v0, /device:TPU:1, one launch (start us, length us, event | category | flops | bytes accessed | tf_op | source)
XLA Modules:
  0.0 70.5 jit_solution(7377736072800968498)
XLA Ops:
  0.6 67.4 %shard_map.77 = (f32[16,32,128]{2,1,0:T(8,128)}, f32[16,32,128]{2,1,0:T(8,128)}) custom-call(f32[16,32,128]{2,1,0:T(8,128)} %f_hbm.1, f32[16,32,128]{2,1,0:T(8,128)} %u_hbm.1, f32[16,32,128]{2,1,0:T(8,128)} %a_hbm.1, f32[16,32,128]{2,1,0:T(8,128)} %bx_hbm.1, f32[16,32,128]{2,1,0:T(8,128)} %by_hbm.1, f32[16,32,128]{2,1,0:T(8,128)} %bz_hbm.1), custom_call_target="tpu_custom_call" | custom-call | tf_op jit(solution)/shard_map/pallas_call | solution.py:817
  68.1 0.0 copy-start
  68.1 1.7 %copy.10 = f32[16,32,128]{2,1,0:T(8,128)} copy(f32[16,32,128]{2,1,0:T(8,128)} %get-tuple-element.4) | data formatting | bytes 524288
  69.8 0.0 copy-done
  69.8 0.7 copy.11
Async XLA Ops:
  68.1 1.7 %copy-start = (f32[16,32,128]{2,1,0:T(8,128)S(1)}, f32[16,32,128]{2,1,0:T(8,128)}, u32[]{:S(2)}) copy-start(f32[16,32,128]{2,1,0:T(8,128)} %get-tuple-element.5) | copy-start | bytes 786436
where the time goes:
time: 70.6 us; the launch traced here: 70.5 us
  Pallas kernels  67.4 us (95%)
  local copies, waits for them, and re-layouts  2.42 us (3%)
    pallas_call x1, Pallas kernels, on_device(): pl.pallas_call(kernel, out_shape=(block, block), in_specs=[pl.BlockSpec(m...  67.4 us
    unnamed x4, local copies, waits for them, and re-layouts  2.42 us

commit v1 on v0

--- a/solution.py
+++ b/solution.py
@@ -84,8 +84,10 @@
     core = lax.rem(gx, 2)
     chip = ((gx // 2) * 4 + gy) * 4 + gz
 
+    near = [[lax.rem(me[d] + (k + GRID[d]), GRID[d]) if k else me[d] for k in (-1, 0, 1)] for d in range(3)]
+
     def nb(o):
-        return tuple(lax.rem(me[d] + (o[d] + GRID[d]), GRID[d]) if o[d] else me[d] for d in range(3))
+        return tuple(near[d][o[d] + 1] for d in range(3))
 
     partner = (gx + 1 - 2 * core, gy, gz)
 
@@ -386,7 +388,7 @@
             dst[p + 1] = total * k0[ID_R if colour == RED else ID_B, p]
             return carry
 
-        lax.fori_loop(start, stop, one_pair, 0, unroll=2)
+        lax.fori_loop(start, stop, one_pair, 0, unroll=4)
 
     half0(RED, u0, r0, 0, 12)
     half0(BLACK, r0, b0, 0, 12)
@@ -406,7 +408,7 @@
         work[pl.ds(32 * p, 32), :] = (red + black)[8:40, :128]
         return carry
 
-    lax.fori_loop(0, 8, restrict0, 0, unroll=2)
+    lax.fori_loop(0, 8, restrict0, 0, unroll=4)
     work2[pl.ds(0, 256), :] = dot(work[pl.ds(0, 256), :], mats[SUM])
     acc = jnp.zeros((16, 128), F32)
     values = []
@@ -501,7 +503,7 @@
             dst[p + 1] = total * k1[ID_R if colour == RED else ID_B, p]
             return carry
 
-        lax.fori_loop(0, 12, one_pair, 0, unroll=6)
+        lax.fori_loop(0, 12, one_pair, 0, unroll=12)
 
     half1(BLACK, r1, b1)
     half1(RED, b1, r1)
@@ -632,7 +634,7 @@
             dst[p + 1] = total * k2[ID_R if colour == RED else ID_B, p]
             return carry
 
-        lax.fori_loop(0, 16, one_pair, 0, unroll=8)
+        lax.fori_loop(0, 16, one_pair, 0, unroll=16)
 
     half2(BLACK, r2, b2)
     half2(RED, b2, r2)
@@ -699,7 +701,7 @@
         black = half_small(BLACK, red, fb4, k4, q8)
         return tuple(red + black)
 
-    done = lax.fori_loop(0, 11, bottom, tuple(r4 + b4))
+    done = lax.fori_loop(0, 11, bottom, tuple(r4 + b4), unroll=11)
     e4 = unpacked(done[:4], done[4:], q8)
 
     def doubled(rows, size):
@@ -775,7 +777,7 @@
         return carry
 
     lax.fori_loop(3, 11, own_black, 0)
-    lax.fori_loop(0, 14, lift_halo, 0, unroll=2)
+    lax.fori_loop(0, 14, lift_halo, 0, unroll=7)
     half0(RED, u1, r0, 0, 12)
     half0(BLACK, r0, b0, 0, 12)
     half0(RED, b0, r0, 1, 11)
@@ -791,7 +793,7 @@
         sol[2 * p + 1] = jnp.where(q_in, black, red)
         return carry
 
-    lax.fori_loop(0, 8, finish, 0, unroll=2)
+    lax.fori_loop(0, 8, finish, 0, unroll=4)
 
 
 def on_device(right_side, initial, alpha, beta_x, beta_y, beta_z):

time: 70.6 us -> 68 us (0.963)
  Pallas kernels: 67.4 us -> 64.7 us
    pallas_call x1, Pallas kernels: 67.4 us -> 64.7 us  [on_device(): pl.pallas_call(kernel, out_shape=(block, block), in_specs=[pl.BlockSpec(m...]
where the time goes in v1:
time: 68 us; the launch traced here: 67.8 us
  Pallas kernels  64.7 us (95%)
  local copies, waits for them, and re-layouts  2.42 us (4%)
    pallas_call x1, Pallas kernels, on_device(): pl.pallas_call(kernel, out_shape=(block, block), in_specs=[pl.BlockSpec(m...  64.7 us
    unnamed x4, local copies, waits for them, and re-layouts  2.42 us

profile of v1, /device:TPU:1, one launch (start us, length us, event | category | flops | bytes accessed | tf_op | source)
XLA Modules:
  0.0 67.8 jit_solution(13632549036018067979)
XLA Ops:
  0.6 64.7 %shard_map.77 = (f32[16,32,128]{2,1,0:T(8,128)}, f32[16,32,128]{2,1,0:T(8,128)}) custom-call(f32[16,32,128]{2,1,0:T(8,128)} %f_hbm.1, f32[16,32,128]{2,1,0:T(8,128)} %u_hbm.1, f32[16,32,128]{2,1,0:T(8,128)} %a_hbm.1, f32[16,32,128]{2,1,0:T(8,128)} %bx_hbm.1, f32[16,32,128]{2,1,0:T(8,128)} %by_hbm.1, f32[16,32,128]{2,1,0:T(8,128)} %bz_hbm.1), custom_call_target="tpu_custom_call" | custom-call | tf_op jit(solution)/shard_map/pallas_call | solution.py:819
  65.4 0.0 copy-start
  65.4 1.7 %copy.10 = f32[16,32,128]{2,1,0:T(8,128)} copy(f32[16,32,128]{2,1,0:T(8,128)} %get-tuple-element.4) | data formatting | bytes 524288
  67.1 0.0 copy-done
  67.1 0.7 %copy.11 = f32[16,32,128]{2,1,0:T(8,128)} copy(f32[16,32,128]{2,1,0:T(8,128)S(1)} %copy-done) | data formatting | bytes 524288
Async XLA Ops:
  65.4 1.7 %copy-start = (f32[16,32,128]{2,1,0:T(8,128)S(1)}, f32[16,32,128]{2,1,0:T(8,128)}, u32[]{:S(2)}) copy-start(f32[16,32,128]{2,1,0:T(8,128)} %get-tuple-element.5) | copy-start | bytes 786436

commit v2 on v1

--- a/solution.py
+++ b/solution.py
@@ -494,7 +494,7 @@
         r1[p + 1] = red * k1[ID_R, p]
         return carry
 
-    lax.fori_loop(0, 12, source1, 0, unroll=4)
+    lax.fori_loop(0, 12, source1, 0, unroll=12)
 
     def half1(colour, src, dst):
         def one_pair(p, carry):
@@ -625,7 +625,7 @@
         r2[p + 1] = red * k2[ID_R, p]
         return carry
 
-    lax.fori_loop(0, 16, source2, 0, unroll=2)
+    lax.fori_loop(0, 16, source2, 0, unroll=16)
 
     def half2(colour, src, dst):
         def one_pair(p, carry):
@@ -647,7 +647,7 @@
         work[pl.ds(pl.multiple_of(32 * p, 32), 32), :] = total + (other - k2[D_B, p] * b2[p + 1])
         return carry
 
-    lax.fori_loop(0, 16, restrict2, 0, unroll=4)
+    lax.fori_loop(0, 16, restrict2, 0, unroll=16)
     work2[pl.ds(0, 512), :] = dot(work[pl.ds(0, 512), :], mats[SUM])
 
     def pack(rows, q):
@@ -745,7 +745,7 @@
         b1[p + 1] = value + work2[pl.ds(pl.multiple_of(32 * p, 32), 32), :]
         return carry
 
-    lax.fori_loop(0, 12, lift1, 0, unroll=4)
+    lax.fori_loop(0, 12, lift1, 0, unroll=12)
     half1(RED, b1, r1)
     half1(BLACK, r1, b1)
     half1(RED, b1, r1)

time: 68 us -> 66.9 us (0.984)
  Pallas kernels: 64.7 us -> 63.7 us
    pallas_call x1, Pallas kernels: 64.7 us -> 63.7 us  [on_device(): pl.pallas_call(kernel, out_shape=(block, block), in_specs=[pl.BlockSpec(m...]
where the time goes in v2:
time: 66.9 us; the launch traced here: 66.8 us
  Pallas kernels  63.7 us (95%)
  local copies, waits for them, and re-layouts  2.42 us (4%)
    pallas_call x1, Pallas kernels, on_device(): pl.pallas_call(kernel, out_shape=(block, block), in_specs=[pl.BlockSpec(m...  63.7 us
    unnamed x4, local copies, waits for them, and re-layouts  2.42 us

profile of v2, /device:TPU:1, one launch (start us, length us, event | category | flops | bytes accessed | tf_op | source)
XLA Modules:
  0.0 66.8 jit_solution(3637900164656206247)
XLA Ops:
  0.6 63.7 %shard_map.77 = (f32[16,32,128]{2,1,0:T(8,128)}, f32[16,32,128]{2,1,0:T(8,128)}) custom-call(f32[16,32,128]{2,1,0:T(8,128)} %f_hbm.1, f32[16,32,128]{2,1,0:T(8,128)} %u_hbm.1, f32[16,32,128]{2,1,0:T(8,128)} %a_hbm.1, f32[16,32,128]{2,1,0:T(8,128)} %bx_hbm.1, f32[16,32,128]{2,1,0:T(8,128)} %by_hbm.1, f32[16,32,128]{2,1,0:T(8,128)} %bz_hbm.1), custom_call_target="tpu_custom_call" | custom-call | tf_op jit(solution)/shard_map/pallas_call | solution.py:819
  64.3 0.0 copy-start
  64.4 1.7 %copy.10 = f32[16,32,128]{2,1,0:T(8,128)} copy(f32[16,32,128]{2,1,0:T(8,128)} %get-tuple-element.4) | data formatting | bytes 524288
  66.1 0.0 copy-done
  66.1 0.7 %copy.11 = f32[16,32,128]{2,1,0:T(8,128)} copy(f32[16,32,128]{2,1,0:T(8,128)S(1)} %copy-done) | data formatting | bytes 524288
Async XLA Ops:
  64.3 1.7 %copy-start = (f32[16,32,128]{2,1,0:T(8,128)S(1)}, f32[16,32,128]{2,1,0:T(8,128)}, u32[]{:S(2)}) copy-start(f32[16,32,128]{2,1,0:T(8,128)} %get-tuple-element.5) | copy-start | bytes 786436

commit v3 on v2

--- a/solution.py
+++ b/solution.py
@@ -369,7 +369,7 @@
         g0[BLACK, p] = jnp.where(q_l0, f_o, f_e)
         return carry
 
-    lax.fori_loop(0, 12, build0, 0, unroll=2)
+    lax.fori_loop(0, 12, build0, 0, unroll=3)
 
     passed_on(1)
     pass_on(2)
@@ -559,7 +559,7 @@
             out.append(total)
         return out
 
-    def place(tiles_of, count):
+    def place(tiles_of, count, batch):
         def one_block(t, carry):
             bx, by = t // 4, lax.rem(t, 4)
             rows = pl.ds(pl.multiple_of(8 * by, 8), 8)
@@ -568,9 +568,9 @@
                     w2[n, 4 * bx + m, rows, :] = value
             return carry
 
-        lax.fori_loop(0, 32, one_block, 0, unroll=4)
-
-    place(lambda side_core, bz, by, k, n: ga[side_core, bz, by, k, n], 4)
+        lax.fori_loop(0, 32, one_block, 0, unroll=batch)
+
+    place(lambda side_core, bz, by, k, n: ga[side_core, bz, by, k, n], 4, 4)
 
     keep_y2 = one(iota((32, 128), 0) != 0)
     keep_z2 = one(lane32 != 0)
@@ -615,7 +615,7 @@
     pair_b.start()
     pair_b.wait()
 
-    place(lambda side_core, bz, by, k, n: gb[side_core, bz * 16 + by * 4 + k], 1)
+    place(lambda side_core, bz, by, k, n: gb[side_core, bz * 16 + by * 4 + k], 1, 16)
 
     def source2(p, carry):
         f_e, f_o = w2[0, 2 * p], w2[0, 2 * p + 1]

time: 66.9 us -> 66.5 us (level)
  no operation moved by 1% of the time
where the time goes in v3:
time: 66.5 us; the launch traced here: 66.3 us
  Pallas kernels  63.2 us (95%)
  local copies, waits for them, and re-layouts  2.42 us (4%)
    pallas_call x1, Pallas kernels, on_device(): pl.pallas_call(kernel, out_shape=(block, block), in_specs=[pl.BlockSpec(m...  63.2 us
    unnamed x4, local copies, waits for them, and re-layouts  2.42 us

profile of v3, /device:TPU:1, one launch (start us, length us, event | category | flops | bytes accessed | tf_op | source)
XLA Modules:
  0.0 66.3 jit_solution(12989709436446812047)
XLA Ops:
  0.6 63.2 %shard_map.77 = (f32[16,32,128]{2,1,0:T(8,128)}, f32[16,32,128]{2,1,0:T(8,128)}) custom-call(f32[16,32,128]{2,1,0:T(8,128)} %f_hbm.1, f32[16,32,128]{2,1,0:T(8,128)} %u_hbm.1, f32[16,32,128]{2,1,0:T(8,128)} %a_hbm.1, f32[16,32,128]{2,1,0:T(8,128)} %bx_hbm.1, f32[16,32,128]{2,1,0:T(8,128)} %by_hbm.1, f32[16,32,128]{2,1,0:T(8,128)} %bz_hbm.1), custom_call_target="tpu_custom_call" | custom-call | tf_op jit(solution)/shard_map/pallas_call | solution.py:819
  63.9 0.0 copy-start
  63.9 1.7 %copy.10 = f32[16,32,128]{2,1,0:T(8,128)} copy(f32[16,32,128]{2,1,0:T(8,128)} %get-tuple-element.4) | data formatting | bytes 524288
  65.6 0.0 copy-done
  65.6 0.7 %copy.11 = f32[16,32,128]{2,1,0:T(8,128)} copy(f32[16,32,128]{2,1,0:T(8,128)S(1)} %copy-done) | data formatting | bytes 524288
Async XLA Ops:
  63.9 1.7 %copy-start = (f32[16,32,128]{2,1,0:T(8,128)S(1)}, f32[16,32,128]{2,1,0:T(8,128)}, u32[]{:S(2)}) copy-start(f32[16,32,128]{2,1,0:T(8,128)} %get-tuple-element.5) | copy-start | bytes 786436
